TPU v7x, 256 devices: a whole 4x4x8 slice. The times are simulated.
256 devices in a mesh: row: 16 (over z, core), col: 16 (over x, y).
Axes of the slice: x: 4, y: 4, z: 8, core: 2. Of those that a mesh axis runs over, the one named last changes fastest.
Arguments:
- events: int32 [52, 1024, 4096], P(None, 'row', 'col'), may hold values 0 or 1
- entry_week: int32 [1024, 4096], P('row', 'col'), may hold values from 0 to 25
- exit_week: int32 [1024, 4096], P('row', 'col'), may hold values from 26 to 52
- log_offset: float32 [1024, 4096], P('row', 'col'), may hold values from -3 to 3
- frailty: float32 [1024, 4096], P('row', 'col'), may hold values from -2 to 2
- kappa_sq: float32 [1024, 4096], P('row', 'col'), may hold values from 0.001 to 0.01
- log_rate: float32 [1], replicated, may hold values from -6 to -4
- shape_rate: float32 [1], replicated, may hold values from 0.5 to 2
Outputs:
- newton_step: float32 [1024, 4096], P('row', 'col')
- residual: float32 [1024, 4096], P('row', 'col')
All inputs are finite; a program needn't handle non-finite values. No bound on the sum of `events` on one device may be relied on, other than what follows from the above.
Results may differ from a plain program's by a relative error of at most 0.0007.
Values sent between devices are 32-bit elements; how exact they have to be, the bound alone decides.
A program may use at most 128 MiB of HBM per device.

v0:
```python
import functools

import jax
import jax.numpy as jnp
from jax import lax
from jax.experimental import pallas as pl
from jax.experimental.pallas import tpu as pltpu
from jax.sharding import PartitionSpec as P


ITERS = 8
TAU = 16.0
MESH = pl.DeviceIdType.MESH
TR, TC = 64, 256
ND = 16
K = 32
GR = 20
EV_PARTS = 4
PIVOT_MIN = 2e-3
f32 = jnp.float32


def iota(shape, dim):
    return lax.broadcasted_iota(jnp.int32, shape, dim)


def seg_transpose(x):
    sub = iota(x.shape, 0) % 4
    seg = iota(x.shape, 1) // 32
    n = x.shape[0]
    out = x
    for d in (1, 2, 3):
        y = jnp.where(sub + d < 4, pltpu.roll(x, n - d, 0), pltpu.roll(x, 4 - d, 0))
        y = pltpu.roll(y, 32 * d, 1)
        out = jnp.where((seg - sub + 4) % 4 == d, y, out)
    return out


def to_groups(tile_of):
    low = iota((8, 128), 0) < 4
    parts = []
    for t in range(TR // 8):
        a, b = tile_of(t, 0), tile_of(t, 1)
        parts.append(jnp.where(low, a, pltpu.roll(b, 4, 0)))
        parts.append(jnp.where(low, pltpu.roll(a, 4, 0), b))
    return seg_transpose(jnp.concatenate(parts, 0))


def kernel(
    mode,
    lr_ref,
    sr_ref,
    ev_hbm,
    en_hbm,
    ex_hbm,
    lo_hbm,
    fr_hbm,
    ka_hbm,
    x_out,
    r_out,
    flag_out,
    ev,
    en,
    ex,
    lo,
    fr,
    ka,
    e_ref,
    hv_rx,
    hh_rx,
    U,
    rx,
    rxv,
    S,
    inv,
    u,
    v,
    pcr,
    Y,
    RHS,
    V,
    RHO,
    AV,
    MK,
    HV,
    GM,
    m1,
    m2,
    g1,
    g2,
    S2,
    OM,
    ORX,
    in_sem,
    hal_send,
    hal_recv,
    rx_send,
    rx_recv,
    rxv_send,
    rxv_recv,
    g_send,
    g_recv,
    o_send,
    o_recv,
):
    i = lax.axis_index("row")
    j = lax.axis_index("col")
    m = j // 2
    up_i, down_i = (i + ND - 1) % ND, (i + 1) % ND
    left_j, right_j = (j + ND - 1) % ND, (j + 1) % ND

    barrier = pltpu.get_barrier_semaphore()

    def hello(a, b):
        pl.semaphore_signal(barrier, inc=1, device_id=(a, b), device_id_type=MESH)

    for d in range(1, ND):
        hello(i, (j + d) % ND)
    for d in range(1, ND):
        hello((i + d) % ND, j)

    @pl.when(j < 2)
    def _():
        for b in range(ND):
            hello(up_i, b)

    @pl.when(j >= ND - 2)
    def _():
        for b in range(ND):
            hello(down_i, b)

    loads = [
        pltpu.make_async_copy(src, dst, in_sem.at[n])
        for n, (src, dst) in enumerate(
            ((fr_hbm, fr), (ex_hbm, ex), (en_hbm, en), (lo_hbm, lo), (ka_hbm, ka))
        )
    ]
    weeks = ev.shape[0] // EV_PARTS
    ev_loads = [
        pltpu.make_async_copy(
            ev_hbm.at[pl.ds(n * weeks, weeks)], ev.at[pl.ds(n * weeks, weeks)], in_sem.at[5 + n]
        )
        for n in range(EV_PARTS)
    ]
    for c in loads + ev_loads:
        c.start()
    for c in loads:
        c.wait()

    rate = jnp.full((1, TC), sr_ref[0], f32)
    scale = jnp.exp(jnp.full((1, TC), lr_ref[0], f32)) / rate
    slope = rate / float(ev.shape[0])
    exposure = scale * (jnp.exp(slope * ex[...].astype(f32)) - jnp.exp(slope * en[...].astype(f32)))
    weight = exposure * jnp.exp(lo[...] + fr[...])
    e_ref[...] = -weight - TAU * (4.0 + ka[...]) * fr[...]
    diag = 2.0 + ka[...] + weight * (1.0 / TAU)

    fill = iota((2, 8, 128), 0) * 0
    for f, value in ((0, 4.0), (1, 0.0)):
        U[f, 0:2] = fill.astype(f32) + value
        U[f, GR - 2 : GR] = fill.astype(f32) + value
    U[0, 2 : GR - 2] = to_groups(
        lambda t, h: diag[8 * t : 8 * t + 8, 128 * h : 128 * h + 128]
    ).reshape(TR // 4, 8, 128)
    part = diag - 2.0
    part = part[:, 0:128] + part[:, 128:256]
    m1[0] = jnp.sum(part.reshape(8, 8, 128), axis=0)

    def field_sends(f):
        out = []
        for d in range(1, ND):
            b = (j + d) % ND
            out.append(
                pltpu.make_async_remote_copy(
                    src_ref=U.at[f, pl.ds(2 * (b // 2), 6)],
                    dst_ref=rx.at[f, j],
                    send_sem=rx_send.at[f],
                    recv_sem=rx_recv.at[f],
                    device_id=(i, b),
                    device_id_type=MESH,
                )
            )
        for first, a, b in (
            (GR - 4, down_i, 0),
            (GR - 4, down_i, 1),
            (2, up_i, ND - 2),
            (2, up_i, ND - 1),
        ):
            out.append(
                pltpu.make_async_remote_copy(
                    src_ref=U.at[f, pl.ds(first, 2)],
                    dst_ref=rxv.at[f, j],
                    send_sem=rxv_send.at[f],
                    recv_sem=rxv_recv.at[f],
                    device_id=(a, b),
                    device_id_type=MESH,
                )
            )
        return out

    def group_sends(src, dst, sem, axis):
        me = j if axis == "col" else i
        return [
            pltpu.make_async_remote_copy(
                src_ref=src,
                dst_ref=dst.at[me],
                send_sem=g_send.at[sem],
                recv_sem=g_recv.at[sem],
                device_id=(i, (j + d) % ND) if axis == "col" else ((i + d) % ND, j),
                device_id_type=MESH,
            )
            for d in range(1, ND)
        ]

    def wait_group(dst, sem):
        whole = pltpu.make_async_remote_copy(
            src_ref=dst.at[pl.ds(0, ND - 1)],
            dst_ref=dst.at[pl.ds(0, ND - 1)],
            send_sem=g_send.at[sem],
            recv_sem=g_recv.at[sem],
            device_id=(i, right_j),
            device_id_type=MESH,
        )
        whole.wait_recv()
        return whole

    def exchange(slot, axis_first):
        first, second = ("row", "col") if axis_first == "row" else ("col", "row")
        me1 = j if first == "col" else i
        me2 = j if second == "col" else i
        for c in group_sends(m1.at[slot], g1.at[slot], 2 * slot, first):
            c.start()
        g1[slot, me1] = m1[slot]
        wait_group(g1.at[slot], 2 * slot)
        m2[slot] = jnp.sum(g1[slot], axis=0)
        for c in group_sends(m2.at[slot], g2.at[slot], 2 * slot + 1, second):
            c.start()
        g2[slot, me2] = m2[slot]
        wait_group(g2.at[slot], 2 * slot + 1)
        return jnp.sum(g2[slot], axis=0)

    pl.semaphore_wait(barrier, 2 * (ND - 1) + 4)

    halos = [
        pltpu.make_async_remote_copy(
            src_ref=src,
            dst_ref=dst,
            send_sem=hal_send.at[n],
            recv_sem=hal_recv.at[n],
            device_id=dev,
            device_id_type=MESH,
        )
        for n, (src, dst, dev) in enumerate(
            (
                (fr.at[pl.ds(TR - 8, 8)], hv_rx.at[0], (down_i, j)),
                (fr.at[pl.ds(0, 8)], hv_rx.at[1], (up_i, j)),
                (fr.at[:, pl.ds(128, 128)], hh_rx.at[0], (i, right_j)),
                (fr.at[:, pl.ds(0, 128)], hh_rx.at[1], (i, left_j)),
            )
        )
    ]
    for c in halos:
        c.start()
    if mode == "fast":
        for c in group_sends(m1.at[0], g1.at[0], 0, "row"):
            c.start()
    for c in field_sends(0):
        c.start()

    en_v, ex_v = en[...], ex[...]
    count = jnp.zeros((TR, TC), jnp.int32)
    for n in range(EV_PARTS):
        ev_loads[n].wait()

        def add_week(w, acc):
            week = w + n * weeks
            at_risk = (week >= en_v) & (week < ex_v)
            return acc + jnp.where(at_risk, ev[week], 0)

        count = lax.fori_loop(0, weeks, add_week, count)
    e_ref[...] = e_ref[...] + count.astype(f32)

    for c in halos:
        c.wait_recv()
    row = iota((TR, 128), 0)
    lane = iota((TR, 128), 1)
    has_up, has_down = jnp.where(i > 0, 1.0, 0.0), jnp.where(i < ND - 1, 1.0, 0.0)
    has_left, has_right = jnp.where(j > 0, 1.0, 0.0), jnp.where(j < ND - 1, 1.0, 0.0)
    halves = []
    for h in (0, 1):
        cols = slice(128 * h, 128 * h + 128)
        here = fr[:, cols]
        above = jnp.where(row == 0, hv_rx[0, 7:8, cols] * has_up, pltpu.roll(here, 1, 0))
        below = jnp.where(row == TR - 1, hv_rx[1, 0:1, cols] * has_down, pltpu.roll(here, TR - 1, 0))
        if h == 0:
            beside_l, beside_r = hh_rx[0] * has_left, fr[:, 128:256]
        else:
            beside_l, beside_r = fr[:, 0:128], hh_rx[1] * has_right
        west = jnp.where(lane == 0, pltpu.roll(beside_l, 1, 1), pltpu.roll(here, 1, 1))
        east = jnp.where(lane == 127, pltpu.roll(beside_r, 127, 1), pltpu.roll(here, 127, 1))
        total = e_ref[:, cols] + TAU * ((below + above) + (east + west))
        halves.append(total * (1.0 / TAU))
    U[1, 2 : GR - 2] = to_groups(lambda t, h: halves[h][8 * t : 8 * t + 8, :]).reshape(TR // 4, 8, 128)
    for c in field_sends(1):
        c.start()

    if mode == "fast":
        g1[0, i] = m1[0]
        wait_group(g1.at[0], 0)
        m2[0] = jnp.sum(g1[0], axis=0)
        for c in group_sends(m2.at[0], g2.at[0], 1, "col"):
            c.start()
        g2[0, j] = m2[0]

    def to_lines(f, dst, outside):
        rx[f, j] = U[f, pl.ds(2 * m, 6)]
        whole = pltpu.make_async_remote_copy(
            src_ref=rx.at[f, pl.ds(0, ND - 1)],
            dst_ref=rx.at[f, pl.ds(0, ND - 1)],
            send_sem=rx_send.at[f],
            recv_sem=rx_recv.at[f],
            device_id=(i, right_j),
            device_id_type=MESH,
        )
        whole.wait_recv()
        beyond = pltpu.make_async_remote_copy(
            src_ref=rxv.at[f],
            dst_ref=rxv.at[f],
            send_sem=rxv_send.at[f],
            recv_sem=rxv_recv.at[f],
            device_id=(i, right_j),
            device_id_type=MESH,
        )

        @pl.when(m == 0)
        def _():
            beyond.wait_recv()
            for b in range(ND):
                rx[f, b, 0:2] = rxv[f, b]

        @pl.when(m == ND // 2 - 1)
        def _():
            beyond.wait_recv()
            for b in range(ND):
                rx[f, b, 4:6] = rxv[f, b]

        for g in range(6):
            S[128 * g : 128 * g + 128] = rx[f, :, g].reshape(128, 128).T
        inside = MK[...] > 0.5
        for k in range(K):
            lines = jnp.concatenate(
                [S[pl.ds(256 * t + k, 8, stride=32), :] for t in range(3)], 0
            )
            dst[k] = jnp.where(inside, lines, outside)

    rows24 = iota((24, 128), 0)
    lanes24 = iota((24, 128), 1)
    lattice_row = TR * i + 8 * (m - 1) + rows24
    MK[...] = jnp.where((lattice_row >= 0) & (lattice_row < TR * ND), 1.0, 0.0)

    to_lines(0, Y, 4.0)

    def after(x):
        return jnp.where(lanes24 == 127, 0.0, pltpu.roll(x, 127, 1))

    def before(x):
        return jnp.where(lanes24 == 0, 0.0, pltpu.roll(x, 1, 1))

    p = 1.0 / Y[0]
    inv[0] = p
    prod = p
    u[0] = prod
    for k in range(1, K - 1):
        p = 1.0 / (Y[k] - p)
        inv[k] = p
        prod = prod * p
        u[k] = prod
    last_u = prod
    q = p
    v[K - 2] = q
    w_u = prod
    for k in range(K - 3, -1, -1):
        p_k = inv[k]
        q = p_k * q
        v[k] = q
        w_u = u[k] + p_k * w_u
        u[k] = w_u
    pivot = 1.0 / (Y[K - 1] - p - after(w_u))
    lo_c = jnp.where(lanes24 == 0, 0.0, last_u) * pivot
    hi_c = after(last_u) * pivot
    pcr[0, 0] = pivot
    for n in range(7):
        s = 1 << n
        d = 1.0 / (1.0 - lo_c * pltpu.roll(hi_c, s, 1) - hi_c * pltpu.roll(lo_c, 128 - s, 1))
        a, b = d * lo_c, d * hi_c
        pcr[n + 1, 0] = d
        pcr[n + 1, 1] = a
        pcr[n + 1, 2] = b
        lo_c = a * pltpu.roll(lo_c, s, 1)
        hi_c = b * pltpu.roll(hi_c, 128 - s, 1)

    to_lines(1, RHS, 0.0)

    def solve(put):
        r = RHS[0]
        f = inv[0] * r
        ends = u[0] * r
        Y[0] = f
        for k in range(1, K - 1):
            r = RHS[k]
            ends = ends + u[k] * r
            f = inv[k] * (r + f)
            Y[k] = f
        x = pcr[0, 0] * (RHS[K - 1] + f + after(ends))
        for n in range(7):
            s = 1 << n
            x = (
                pcr[n + 1, 0] * x
                + pcr[n + 1, 1] * pltpu.roll(x, s, 1)
                + pcr[n + 1, 2] * pltpu.roll(x, 128 - s, 1)
            )
        for k in range(K - 3, -1, -1):
            f = Y[k] + inv[k] * f
            Y[k] = f
        prev = before(x)
        put(K - 1, x)
        for k in range(K - 2, -1, -1):
            put(k, Y[k] + (u[k] * prev + v[k] * x))

    def across(z):
        return MK[...] * (2.0 * z - (pltpu.roll(z, 1, 0) + pltpu.roll(z, 23, 0)))

    own = slice(8, 16)
    sub8 = iota((8, 128), 0)
    lane8 = iota((8, 128), 1)

    if mode == "fast":
        wait_group(g2.at[0], 1)
        mean = jnp.sum(jnp.sum(g2[0], axis=0), axis=(0, 1), keepdims=True) * (
            1.0 / float(TR * TC * ND * ND)
        )
        HV[...] = jnp.broadcast_to(0.5 * mean, (24, 128))
        zero = jnp.zeros((24, 128), f32)
        for n in (0, 1):
            for k in range(K):
                V[n, k] = zero
                RHO[n, k] = zero[own]

        def basis(it, _):
            w = jnp.where(it == 0, 1.0, HV[...])
            twice = jnp.where(it >= 2, 2.0, 1.0)

            def put(k, x):
                vec = twice * (x * w - V[it + 1, k]) - V[it, k]
                rho = twice * (RHS[k, own] * w[own] - RHO[it + 1, k]) - RHO[it, k]
                V[it + 2, k] = vec
                RHO[it + 2, k] = rho
                tv = across(vec)
                AV[it, k] = rho + tv[own]
                RHS[k] = tv

            solve(put)

            def dots(n, _):
                acc_a = [jnp.zeros((8, 128), f32)] * 4
                acc_n = [jnp.zeros((8, 128), f32)] * 4
                for k in range(K):
                    vec = V[it + 2, k, own]
                    acc_a[k % 4] = acc_a[k % 4] + vec * AV[n, k]
                    acc_n[k % 4] = acc_n[k % 4] + vec * RHO[n + 2, k]
                for first, acc in ((0, acc_a), (64, acc_n)):
                    total = jnp.sum((acc[0] + acc[1]) + (acc[2] + acc[3]), axis=0, keepdims=True)
                    GM[pl.ds(first + 56 - 8 * it + n, 1), :] = total
                    GM[pl.ds(first + 56 - 8 * n + it, 1), :] = total
                return 0

            lax.fori_loop(0, it + 1, dots, 0)
            return 0

        lax.fori_loop(0, ITERS, basis, 0)
        m1[1] = jnp.sum(GM[...].T.reshape(16, 8, 128), axis=0)
        total = exchange(1, "col")
        flat = jnp.sum(total, axis=0, keepdims=True)
        mat = pltpu.roll(jnp.broadcast_to(flat, (8, 128)), 0, 1, stride=8, stride_axis=0)
        worst = jnp.full((8, 1), 1.0, f32)
        diag0 = jnp.sum(jnp.where(lane8 == sub8 + 56, mat, 0.0), axis=1, keepdims=True)
        for n in range(ITERS):
            row_n = jnp.sum(jnp.where(sub8 == n, mat, 0.0), axis=0, keepdims=True)
            col_n = jnp.sum(jnp.where(lane8 == 56 + n, mat, 0.0), axis=1, keepdims=True)
            piv = jnp.sum(jnp.where(sub8[:, 0:1] == n, col_n, 0.0), axis=0, keepdims=True)
            first = jnp.sum(jnp.where(sub8[:, 0:1] == n, diag0, 0.0), axis=0, keepdims=True)
            worst = jnp.minimum(worst, jnp.broadcast_to(piv / first, (8, 1)))
            scaled = row_n / piv
            mat = jnp.where(sub8 == n, jnp.broadcast_to(scaled, (8, 128)), mat - col_n * scaled)
        coef = jnp.sum(jnp.where(lane8 == 120, mat, 0.0), axis=1, keepdims=True)
        coef = jnp.broadcast_to(coef, (8, 128))
        odd = j % 2
        coef = coef * jnp.where(odd == 1, -TAU, 1.0)
        base = jnp.where(odd == 1, TAU, 0.0)
        flag_out[...] = jnp.broadcast_to(worst, (8, 128))
        weights = [jnp.broadcast_to(coef[n : n + 1, :], (8, 128)) for n in range(ITERS)]

        @pl.when(odd == 0)
        def _():
            for k in range(K):
                acc = weights[0] * V[2, k, own]
                for n in range(1, ITERS):
                    acc = acc + weights[n] * V[n + 2, k, own]
                S2[pl.ds(k, 8, stride=32), :] = acc

        @pl.when(odd == 1)
        def _():
            for k in range(K):
                acc = weights[0] * AV[0, k]
                for n in range(1, ITERS):
                    acc = acc + weights[n] * AV[n, k]
                S2[pl.ds(k, 8, stride=32), :] = acc + base * RHO[2, k]

    else:
        zero = jnp.zeros((24, 128), f32)
        for n in (3, 4, 5):
            for k in range(K):
                V[n, k] = zero

        def iterate(it, carry):
            gamma_old, alpha_old = carry
            acc = [jnp.zeros((8, 128), f32)] * 4

            def put(k, x):
                r = RHS[k]
                w = MK[...] * r + across(x)
                V[2, k] = x
                V[6, k] = w
                acc[k % 2] = acc[k % 2] + x[own] * r[own]
                acc[2 + k % 2] = acc[2 + k % 2] + x[own] * w[own]

            solve(put)
            gam = jnp.sum(acc[0] + acc[1], axis=0, keepdims=True)
            mu = jnp.sum(acc[2] + acc[3], axis=0, keepdims=True)
            m1[it] = jnp.where(sub8 == 0, gam, jnp.where(sub8 == 1, mu, 0.0))
            total = jnp.sum(exchange(it, "col"), axis=1, keepdims=True)
            gamma = total[0:1]
            mu = total[1:2]
            beta = jnp.where(it == 0, 0.0, gamma / gamma_old)
            alpha = gamma / (mu - beta * gamma / alpha_old)
            for k in range(K):
                p = V[2, k] + beta * V[3, k]
                s = V[6, k] + beta * V[4, k]
                V[3, k] = p
                V[4, k] = s
                V[5, k] = V[5, k] + alpha * p
                RHS[k] = RHS[k] - alpha * s
            return gamma, alpha

        one = jnp.ones((1, 1), f32)
        lax.fori_loop(0, ITERS, iterate, (one, one))
        odd = j % 2
        flag_out[...] = jnp.ones((8, 128), f32)

        @pl.when(odd == 0)
        def _():
            for k in range(K):
                S2[pl.ds(k, 8, stride=32), :] = V[5, k, own]

        @pl.when(odd == 1)
        def _():
            for k in range(K):
                S2[pl.ds(k, 8, stride=32), :] = TAU * RHS[k, own]

    for g in range(2):
        OM[:, g] = S2[128 * g : 128 * g + 128].T.reshape(ND, 8, 128)
    for d in range(1, ND):
        b = (j + d) % ND
        pltpu.make_async_remote_copy(
            src_ref=OM.at[b],
            dst_ref=ORX.at[j],
            send_sem=o_send,
            recv_sem=o_recv,
            device_id=(i, b),
            device_id_type=MESH,
        ).start()
    ORX[j] = OM[j]
    back = pltpu.make_async_remote_copy(
        src_ref=ORX.at[pl.ds(0, ND - 1)],
        dst_ref=ORX.at[pl.ds(0, ND - 1)],
        send_sem=o_send,
        recv_sem=o_recv,
        device_id=(i, right_j),
        device_id_type=MESH,
    )
    back.wait_recv()
    low = iota((8, 128), 0) < 4
    for which, out in ((0, x_out), (1, r_out)):
        groups = jnp.concatenate([ORX[2 * t + which, g] for t in range(TR // 8) for g in range(2)], 0)
        groups = seg_transpose(groups)
        for t in range(TR // 8):
            a = groups[16 * t : 16 * t + 8]
            b = groups[16 * t + 8 : 16 * t + 16]
            out[8 * t : 8 * t + 8, 0:128] = jnp.where(low, a, pltpu.roll(b, 4, 0))
            out[8 * t : 8 * t + 8, 128:256] = jnp.where(low, pltpu.roll(a, 4, 0), b)

    back.wait_send()
    for c in halos:
        c.wait_send()
    for f in (0, 1):
        pltpu.make_async_remote_copy(
            src_ref=rx.at[f, pl.ds(0, ND - 1)],
            dst_ref=rx.at[f, pl.ds(0, ND - 1)],
            send_sem=rx_send.at[f],
            recv_sem=rx_recv.at[f],
            device_id=(i, right_j),
            device_id_type=MESH,
        ).wait_send()
        pltpu.make_async_remote_copy(
            src_ref=rxv.at[f, pl.ds(0, 4)],
            dst_ref=rxv.at[f, pl.ds(0, 4)],
            send_sem=rxv_send.at[f],
            recv_sem=rxv_recv.at[f],
            device_id=(i, right_j),
            device_id_type=MESH,
        ).wait_send()
    for slot in range(2 if mode == "fast" else ITERS):
        for half, dst in ((0, g1), (1, g2)):
            pltpu.make_async_remote_copy(
                src_ref=dst.at[slot, pl.ds(0, ND - 1)],
                dst_ref=dst.at[slot, pl.ds(0, ND - 1)],
                send_sem=g_send.at[2 * slot + half],
                recv_sem=g_recv.at[2 * slot + half],
                device_id=(i, right_j),
                device_id_type=MESH,
            ).wait_send()


def run(mode, events, entry_week, exit_week, log_offset, frailty, kappa_sq, log_rate, shape_rate):
    slots = 2 if mode == "fast" else ITERS
    vm = pltpu.VMEM
    dma = pltpu.SemaphoreType.DMA
    return pl.pallas_call(
        functools.partial(kernel, mode),
        out_shape=(
            jax.ShapeDtypeStruct((TR, TC), f32),
            jax.ShapeDtypeStruct((TR, TC), f32),
            jax.ShapeDtypeStruct((8, 128), f32),
        ),
        in_specs=[pl.BlockSpec(memory_space=pltpu.SMEM)] * 2
        + [pl.BlockSpec(memory_space=pl.ANY)] * 6,
        out_specs=(pl.BlockSpec(memory_space=pltpu.VMEM),) * 3,
        scratch_shapes=[
            vm(events.shape, jnp.int32),
            vm((TR, TC), jnp.int32),
            vm((TR, TC), jnp.int32),
            vm((TR, TC), f32),
            vm((TR, TC), f32),
            vm((TR, TC), f32),
            vm((TR, TC), f32),
            vm((2, 8, TC), f32),
            vm((2, TR, 128), f32),
            vm((2, GR, 8, 128), f32),
            vm((2, ND, 6, 8, 128), f32),
            vm((2, ND, 2, 8, 128), f32),
            vm((768, 128), f32),
            vm((K, 24, 128), f32),
            vm((K, 24, 128), f32),
            vm((K, 24, 128), f32),
            vm((8, 3, 24, 128), f32),
            vm((K, 24, 128), f32),
            vm((K, 24, 128), f32),
            vm((ITERS + 2, K, 24, 128), f32),
            vm((ITERS + 2, K, 8, 128), f32),
            vm((ITERS, K, 8, 128), f32),
            vm((24, 128), f32),
            vm((24, 128), f32),
            vm((128, 128), f32),
            vm((slots, 8, 128), f32),
            vm((slots, 8, 128), f32),
            vm((slots, ND, 8, 128), f32),
            vm((slots, ND, 8, 128), f32),
            vm((256, 128), f32),
            vm((ND, 2, 8, 128), f32),
            vm((ND, 2, 8, 128), f32),
            dma((5 + EV_PARTS,)),
            dma((4,)),
            dma((4,)),
            dma((2,)),
            dma((2,)),
            dma((2,)),
            dma((2,)),
            dma((2 * slots,)),
            dma((2 * slots,)),
            dma,
            dma,
        ],
        compiler_params=pltpu.CompilerParams(
            collective_id=0 if mode == "fast" else 1,
            has_side_effects=True,
            vmem_limit_bytes=40 * 2**20,
        ),
        name="newton_" + mode,
    )(log_rate, shape_rate, events, entry_week, exit_week, log_offset, frailty, kappa_sq)


def per_device(*args):
    step, residual, flag = run("fast", *args)
    return lax.cond(
        flag[0, 0] > PIVOT_MIN,
        lambda: (step, residual),
        lambda: tuple(run("cg", *args)[:2]),
    )


def solution(mesh):
    tile = P("row", "col")
    return jax.shard_map(
        per_device,
        mesh=mesh,
        in_specs=(P(None, "row", "col"), tile, tile, tile, tile, tile, P(), P()),
        out_specs=(tile, tile),
        check_vma=False,
    )
```

profile of v0, /device:TPU:1, one launch (start us, length us, event | category | flops | bytes accessed | tf_op | source)
XLA Modules:
  0.0 59.1 jit_solution(18047622247553843659)
XLA Ops:
  0.6 0.0 copy-start.5
  0.6 0.0 copy-start.4
  0.7 0.0 copy-start.3
  0.7 0.0 copy-start.2
  0.7 0.0 copy-start.1
  0.7 0.0 copy-start
  2.5 54.1 %newton_fast.1 = (f32[64,256]{1,0:T(8,128)S(1)}, f32[64,256]{1,0:T(8,128)S(1)}, f32[8,128]{1,0:T(8,128)S(1)}) custom-call(f32[1]{0:T(128)S(6)} %copy.16.lr_ref, f32[1]{0:T(128)S(6)} %copy.17.sr_ref, s32[52,64,256]{2,1,0:T(8,128)} %ev_hbm.1, s32[64,256]{1,0:T(8,128)} %en_hbm.1, s32[64,256]{1,0:T(8,128)} %ex_hbm.1, f32[64,256]{1,0:T(8,128)} %lo_hbm.1, ...), custom_call_target="tpu_custom_call" | custom-call | tf_op jit(solution)/shard_map/newton_fast/pallas_call | solution.py:638
  56.6 0.5 slice.3
  57.7 0.0 copy-done.5
  57.7 0.0 copy-done.4
  57.8 0.0 copy-done.3
  57.8 0.0 copy-done.2
  57.8 0.0 copy-done.1
  57.8 0.0 copy-done
  57.8 0.6 %copy.18 = f32[64,256]{1,0:T(8,128)} copy(f32[64,256]{1,0:T(8,128)S(1)} %get-tuple-element.44) | data formatting | bytes 131072
  58.4 0.6 %copy.19 = f32[64,256]{1,0:T(8,128)} copy(f32[64,256]{1,0:T(8,128)S(1)} %get-tuple-element.45) | data formatting | bytes 131072
  (1 shorter events, 0.0 us)
Async XLA Ops:
  0.6 57.1 %copy-start.5 = (f32[64,256]{1,0:T(8,128)S(1)}, f32[64,256]{1,0:T(8,128)}, u32[]{:S(2)}) copy-start(f32[64,256]{1,0:T(8,128)} %ka_hbm.1) | copy-start | bytes 196612
  0.6 57.1 %copy-start.4 = (f32[64,256]{1,0:T(8,128)S(1)}, f32[64,256]{1,0:T(8,128)}, u32[]{:S(2)}) copy-start(f32[64,256]{1,0:T(8,128)} %fr_hbm.1) | copy-start | bytes 196612
  0.7 57.1 %copy-start.3 = (f32[64,256]{1,0:T(8,128)S(1)}, f32[64,256]{1,0:T(8,128)}, u32[]{:S(2)}) copy-start(f32[64,256]{1,0:T(8,128)} %lo_hbm.1) | copy-start | bytes 196612
  0.7 57.1 %copy-start.2 = (s32[64,256]{1,0:T(8,128)S(1)}, s32[64,256]{1,0:T(8,128)}, u32[]{:S(2)}) copy-start(s32[64,256]{1,0:T(8,128)} %ex_hbm.1) | copy-start | bytes 196612
  0.7 57.1 %copy-start.1 = (s32[64,256]{1,0:T(8,128)S(1)}, s32[64,256]{1,0:T(8,128)}, u32[]{:S(2)}) copy-start(s32[64,256]{1,0:T(8,128)} %en_hbm.1) | copy-start | bytes 196612
  0.7 57.1 %copy-start = (s32[52,64,256]{2,1,0:T(8,128)S(1)}, s32[52,64,256]{2,1,0:T(8,128)}, u32[]{:S(2)}) copy-start(s32[52,64,256]{2,1,0:T(8,128)} %ev_hbm.1) | copy-start | bytes 10223620
where the time goes:
time: 59.2 us; the launch traced here: 59.1 us
  Pallas kernels  54.1 us (91%)
  between operations  3.18 us (5%)
  local copies, waits for them, and re-layouts  1.8 us (3%)
    pallas_call x1, Pallas kernels, run(): pl.pallas_call(functools.partial(kernel, mode), out_shape=(jax.ShapeDtype...  54.1 us
    unnamed x14, local copies, waits for them, and re-layouts  1.29 us

commit v1 on v0

--- a/solution.py
+++ b/solution.py
@@ -48,8 +48,8 @@
 
 def kernel(
     mode,
-    lr_ref,
-    sr_ref,
+    lr_hbm,
+    sr_hbm,
     ev_hbm,
     en_hbm,
     ex_hbm,
@@ -59,6 +59,8 @@
     x_out,
     r_out,
     flag_out,
+    lr_ref,
+    sr_ref,
     ev,
     en,
     ex,
@@ -102,10 +104,16 @@
     g_recv,
     o_send,
     o_recv,
+    s_send,
+    s_recv,
 ):
     i = lax.axis_index("row")
     j = lax.axis_index("col")
-    m = j // 2
+    plane, core = i // 2, i % 2
+    m = j % 8
+    block = 2 * plane + j // 8
+    other = i + 1 - 2 * core
+    home = block == i
     up_i, down_i = (i + ND - 1) % ND, (i + 1) % ND
     left_j, right_j = (j + ND - 1) % ND, (j + 1) % ND
 
@@ -118,27 +126,48 @@
         hello(i, (j + d) % ND)
     for d in range(1, ND):
         hello((i + d) % ND, j)
-
-    @pl.when(j < 2)
+    for d in range(8):
+        hello(other, 8 * core + d)
+
+    @pl.when(jnp.logical_not(home))
     def _():
         for b in range(ND):
-            hello(up_i, b)
-
-    @pl.when(j >= ND - 2)
+            hello(other, b)
+
+    ghost_first = (core == 0) & (m == 0)
+    ghost_last = (core == 1) & (m == 7)
+    ghost_from = (block + jnp.where(core == 0, ND - 1, 1)) % ND
+    below_dev = (2 * (down_i // 2), 8 * (down_i % 2))
+    above_dev = (2 * (up_i // 2) + 1, 8 * (up_i % 2) + 7)
+    below_self = (below_dev[0] == i) & (below_dev[1] == j)
+    above_self = (above_dev[0] == i) & (above_dev[1] == j)
+
+    @pl.when(ghost_first | ghost_last)
     def _():
         for b in range(ND):
-            hello(down_i, b)
+
+            @pl.when(jnp.logical_not((ghost_from == i) & (j == b)))
+            def _():
+                hello(ghost_from, b)
 
     loads = [
         pltpu.make_async_copy(src, dst, in_sem.at[n])
         for n, (src, dst) in enumerate(
-            ((fr_hbm, fr), (ex_hbm, ex), (en_hbm, en), (lo_hbm, lo), (ka_hbm, ka))
+            (
+                (fr_hbm, fr),
+                (ex_hbm, ex),
+                (en_hbm, en),
+                (lo_hbm, lo),
+                (ka_hbm, ka),
+                (lr_hbm, lr_ref),
+                (sr_hbm, sr_ref),
+            )
         )
     ]
     weeks = ev.shape[0] // EV_PARTS
     ev_loads = [
         pltpu.make_async_copy(
-            ev_hbm.at[pl.ds(n * weeks, weeks)], ev.at[pl.ds(n * weeks, weeks)], in_sem.at[5 + n]
+            ev_hbm.at[pl.ds(n * weeks, weeks)], ev.at[pl.ds(n * weeks, weeks)], in_sem.at[7 + n]
         )
         for n in range(EV_PARTS)
     ]
@@ -166,80 +195,99 @@
     part = part[:, 0:128] + part[:, 128:256]
     m1[0] = jnp.sum(part.reshape(8, 8, 128), axis=0)
 
-    def field_sends(f):
-        out = []
-        for d in range(1, ND):
-            b = (j + d) % ND
-            out.append(
+    def send_field(f):
+        for q in (0, 1):
+            for d in range(8):
+                a = (m + d) % 8
+                to = core if q == 0 else 1 - core
+                src = U.at[f, pl.ds(2 * a + 3 * to, 3)]
+
+                def start():
+                    pltpu.make_async_remote_copy(
+                        src_ref=src,
+                        dst_ref=rx.at[f, j],
+                        send_sem=rx_send.at[f],
+                        recv_sem=rx_recv.at[f],
+                        device_id=(2 * plane + to, 8 * core + a),
+                        device_id_type=MESH,
+                    ).start()
+
+                if q == 0 and d == 0:
+                    pl.when(jnp.logical_not(home))(start)
+                else:
+                    start()
+        for first, to, here in ((GR - 4, below_dev, below_self), (2, above_dev, above_self)):
+            src = U.at[f, pl.ds(first, 2)]
+
+            @pl.when(jnp.logical_not(here))
+            def _():
                 pltpu.make_async_remote_copy(
-                    src_ref=U.at[f, pl.ds(2 * (b // 2), 6)],
-                    dst_ref=rx.at[f, j],
-                    send_sem=rx_send.at[f],
-                    recv_sem=rx_recv.at[f],
-                    device_id=(i, b),
-                    device_id_type=MESH,
-                )
-            )
-        for first, a, b in (
-            (GR - 4, down_i, 0),
-            (GR - 4, down_i, 1),
-            (2, up_i, ND - 2),
-            (2, up_i, ND - 1),
-        ):
-            out.append(
-                pltpu.make_async_remote_copy(
-                    src_ref=U.at[f, pl.ds(first, 2)],
+                    src_ref=src,
                     dst_ref=rxv.at[f, j],
                     send_sem=rxv_send.at[f],
                     recv_sem=rxv_recv.at[f],
-                    device_id=(a, b),
+                    device_id=to,
                     device_id_type=MESH,
-                )
-            )
-        return out
+                ).start()
+
+    def bytes_of(ref, send, recv):
+        return pltpu.make_async_remote_copy(
+            src_ref=ref,
+            dst_ref=ref,
+            send_sem=send,
+            recv_sem=recv,
+            device_id=(i, right_j),
+            device_id_type=MESH,
+        )
+
+    def one_less(cond, ref, count, send, recv, act):
+        @pl.when(cond)
+        def _():
+            act(bytes_of(ref.at[pl.ds(0, count - 1)], send, recv))
+
+        @pl.when(jnp.logical_not(cond))
+        def _():
+            act(bytes_of(ref.at[pl.ds(0, count)], send, recv))
+
+    def wait_recv(c):
+        c.wait_recv()
+
+    def wait_send(c):
+        c.wait_send()
 
     def group_sends(src, dst, sem, axis):
-        me = j if axis == "col" else i
-        return [
+        if axis == "col":
+            me, to = j, [(i, (j + d) % ND) for d in range(1, ND)]
+        elif axis == "row":
+            me, to = i, [((i + d) % ND, j) for d in range(1, ND)]
+        else:
+            me, to = plane, [((i + 2 * d) % ND, j) for d in range(1, ND // 2)]
+        for dev in to:
             pltpu.make_async_remote_copy(
                 src_ref=src,
                 dst_ref=dst.at[me],
                 send_sem=g_send.at[sem],
                 recv_sem=g_recv.at[sem],
-                device_id=(i, (j + d) % ND) if axis == "col" else ((i + d) % ND, j),
+                device_id=dev,
                 device_id_type=MESH,
-            )
-            for d in range(1, ND)
-        ]
-
-    def wait_group(dst, sem):
-        whole = pltpu.make_async_remote_copy(
-            src_ref=dst.at[pl.ds(0, ND - 1)],
-            dst_ref=dst.at[pl.ds(0, ND - 1)],
-            send_sem=g_send.at[sem],
-            recv_sem=g_recv.at[sem],
-            device_id=(i, right_j),
-            device_id_type=MESH,
-        )
-        whole.wait_recv()
-        return whole
-
-    def exchange(slot, axis_first):
-        first, second = ("row", "col") if axis_first == "row" else ("col", "row")
-        me1 = j if first == "col" else i
-        me2 = j if second == "col" else i
-        for c in group_sends(m1.at[slot], g1.at[slot], 2 * slot, first):
-            c.start()
-        g1[slot, me1] = m1[slot]
-        wait_group(g1.at[slot], 2 * slot)
+            ).start()
+        dst[me] = src[...]
+
+    def group_bytes(dst, sem, count):
+        return bytes_of(dst.at[pl.ds(0, count - 1)], g_send.at[sem], g_recv.at[sem])
+
+    def exchange(slot):
+        group_sends(m1.at[slot], g1.at[slot], 2 * slot, "col")
+        group_bytes(g1.at[slot], 2 * slot, ND).wait_recv()
         m2[slot] = jnp.sum(g1[slot], axis=0)
-        for c in group_sends(m2.at[slot], g2.at[slot], 2 * slot + 1, second):
-            c.start()
-        g2[slot, me2] = m2[slot]
-        wait_group(g2.at[slot], 2 * slot + 1)
-        return jnp.sum(g2[slot], axis=0)
-
-    pl.semaphore_wait(barrier, 2 * (ND - 1) + 4)
+        group_sends(m2.at[slot], g2.at[slot], 2 * slot + 1, "plane")
+        group_bytes(g2.at[slot], 2 * slot + 1, ND // 2).wait_recv()
+        return jnp.sum(g2[slot, 0 : ND // 2], axis=0)
+
+    greeted = 2 * (ND - 1) + 8 + 2
+    greeted = greeted + jnp.where(home, 0, ND)
+    greeted = greeted - jnp.where(below_self, 1, 0) - jnp.where(above_self, 1, 0)
+    pl.semaphore_wait(barrier, greeted)
 
     halos = [
         pltpu.make_async_remote_copy(
@@ -262,10 +310,8 @@
     for c in halos:
         c.start()
     if mode == "fast":
-        for c in group_sends(m1.at[0], g1.at[0], 0, "row"):
-            c.start()
-    for c in field_sends(0):
-        c.start()
+        group_sends(m1.at[0], g1.at[0], 0, "row")
+    send_field(0)
 
     en_v, ex_v = en[...], ex[...]
     count = jnp.zeros((TR, TC), jnp.int32)
@@ -301,61 +347,57 @@
         total = e_ref[:, cols] + TAU * ((below + above) + (east + west))
         halves.append(total * (1.0 / TAU))
     U[1, 2 : GR - 2] = to_groups(lambda t, h: halves[h][8 * t : 8 * t + 8, :]).reshape(TR // 4, 8, 128)
-    for c in field_sends(1):
-        c.start()
+    send_field(1)
 
     if mode == "fast":
-        g1[0, i] = m1[0]
-        wait_group(g1.at[0], 0)
+        group_bytes(g1.at[0], 0, ND).wait_recv()
         m2[0] = jnp.sum(g1[0], axis=0)
-        for c in group_sends(m2.at[0], g2.at[0], 1, "col"):
-            c.start()
-        g2[0, j] = m2[0]
+        group_sends(m2.at[0], g2.at[0], 1, "col")
 
     def to_lines(f, dst, outside):
-        rx[f, j] = U[f, pl.ds(2 * m, 6)]
-        whole = pltpu.make_async_remote_copy(
-            src_ref=rx.at[f, pl.ds(0, ND - 1)],
-            dst_ref=rx.at[f, pl.ds(0, ND - 1)],
-            send_sem=rx_send.at[f],
-            recv_sem=rx_recv.at[f],
-            device_id=(i, right_j),
-            device_id_type=MESH,
-        )
-        whole.wait_recv()
-        beyond = pltpu.make_async_remote_copy(
-            src_ref=rxv.at[f],
-            dst_ref=rxv.at[f],
-            send_sem=rxv_send.at[f],
-            recv_sem=rxv_recv.at[f],
-            device_id=(i, right_j),
-            device_id_type=MESH,
-        )
-
-        @pl.when(m == 0)
+        @pl.when(home)
         def _():
-            beyond.wait_recv()
-            for b in range(ND):
-                rx[f, b, 0:2] = rxv[f, b]
-
-        @pl.when(m == ND // 2 - 1)
-        def _():
-            beyond.wait_recv()
-            for b in range(ND):
-                rx[f, b, 4:6] = rxv[f, b]
-
-        for g in range(6):
-            S[128 * g : 128 * g + 128] = rx[f, :, g].reshape(128, 128).T
+            rx[f, j] = U[f, pl.ds(2 * m + 3 * core, 3)]
+
+        one_less(home, rx.at[f], ND, rx_send.at[f], rx_recv.at[f], wait_recv)
+
+        def ghosts(first, own_first, cond):
+            @pl.when(cond)
+            def _():
+                self_too = ghost_from == i
+
+                @pl.when(self_too)
+                def _():
+                    rxv[f, j] = U[f, pl.ds(own_first, 2)]
+
+                one_less(self_too, rxv.at[f], ND, rxv_send.at[f], rxv_recv.at[f], wait_recv)
+                for b in range(ND):
+                    rx[f, b, first : first + 2] = rxv[f, b]
+
+        ghosts(0, GR - 4, ghost_first)
+        ghosts(1, 2, ghost_last)
+        for g in range(3):
+            at = pl.ds(384 * core + 128 * g, 128)
+            S[f, at] = rx[f, :, g].reshape(128, 128).T
+            pltpu.make_async_remote_copy(
+                src_ref=S.at[f, at],
+                dst_ref=S.at[f, at],
+                send_sem=s_send.at[f],
+                recv_sem=s_recv.at[f],
+                device_id=(other, j),
+                device_id_type=MESH,
+            ).start()
+        bytes_of(S.at[f, pl.ds(0, 384)], s_send.at[f], s_recv.at[f]).wait_recv()
         inside = MK[...] > 0.5
         for k in range(K):
             lines = jnp.concatenate(
-                [S[pl.ds(256 * t + k, 8, stride=32), :] for t in range(3)], 0
+                [S[f, pl.ds(256 * t + k, 8, stride=32), :] for t in range(3)], 0
             )
             dst[k] = jnp.where(inside, lines, outside)
 
     rows24 = iota((24, 128), 0)
     lanes24 = iota((24, 128), 1)
-    lattice_row = TR * i + 8 * (m - 1) + rows24
+    lattice_row = 2 * TR * plane + 8 * (j - 1) + rows24
     MK[...] = jnp.where((lattice_row >= 0) & (lattice_row < TR * ND), 1.0, 0.0)
 
     to_lines(0, Y, 4.0)
@@ -435,7 +477,7 @@
     lane8 = iota((8, 128), 1)
 
     if mode == "fast":
-        wait_group(g2.at[0], 1)
+        group_bytes(g2.at[0], 1, ND).wait_recv()
         mean = jnp.sum(jnp.sum(g2[0], axis=0), axis=(0, 1), keepdims=True) * (
             1.0 / float(TR * TC * ND * ND)
         )
@@ -479,7 +521,7 @@
 
         lax.fori_loop(0, ITERS, basis, 0)
         m1[1] = jnp.sum(GM[...].T.reshape(16, 8, 128), axis=0)
-        total = exchange(1, "col")
+        total = exchange(1)
         flat = jnp.sum(total, axis=0, keepdims=True)
         mat = pltpu.roll(jnp.broadcast_to(flat, (8, 128)), 0, 1, stride=8, stride_axis=0)
         worst = jnp.full((8, 1), 1.0, f32)
@@ -494,10 +536,10 @@
             mat = jnp.where(sub8 == n, jnp.broadcast_to(scaled, (8, 128)), mat - col_n * scaled)
         coef = jnp.sum(jnp.where(lane8 == 120, mat, 0.0), axis=1, keepdims=True)
         coef = jnp.broadcast_to(coef, (8, 128))
-        odd = j % 2
+        odd = core
         coef = coef * jnp.where(odd == 1, -TAU, 1.0)
         base = jnp.where(odd == 1, TAU, 0.0)
-        flag_out[...] = jnp.broadcast_to(worst, (8, 128))
+        flag_out[0] = jnp.where(jnp.min(worst) > PIVOT_MIN, 1, 0)
         weights = [jnp.broadcast_to(coef[n : n + 1, :], (8, 128)) for n in range(ITERS)]
 
         @pl.when(odd == 0)
@@ -538,7 +580,7 @@
             gam = jnp.sum(acc[0] + acc[1], axis=0, keepdims=True)
             mu = jnp.sum(acc[2] + acc[3], axis=0, keepdims=True)
             m1[it] = jnp.where(sub8 == 0, gam, jnp.where(sub8 == 1, mu, 0.0))
-            total = jnp.sum(exchange(it, "col"), axis=1, keepdims=True)
+            total = jnp.sum(exchange(it), axis=1, keepdims=True)
             gamma = total[0:1]
             mu = total[1:2]
             beta = jnp.where(it == 0, 0.0, gamma / gamma_old)
@@ -554,8 +596,8 @@
 
         one = jnp.ones((1, 1), f32)
         lax.fori_loop(0, ITERS, iterate, (one, one))
-        odd = j % 2
-        flag_out[...] = jnp.ones((8, 128), f32)
+        odd = core
+        flag_out[0] = 1
 
         @pl.when(odd == 0)
         def _():
@@ -569,26 +611,30 @@
 
     for g in range(2):
         OM[:, g] = S2[128 * g : 128 * g + 128].T.reshape(ND, 8, 128)
-    for d in range(1, ND):
+    slot = 2 * m + core
+    for d in range(ND):
         b = (j + d) % ND
-        pltpu.make_async_remote_copy(
-            src_ref=OM.at[b],
-            dst_ref=ORX.at[j],
-            send_sem=o_send,
-            recv_sem=o_recv,
-            device_id=(i, b),
-            device_id_type=MESH,
-        ).start()
-    ORX[j] = OM[j]
-    back = pltpu.make_async_remote_copy(
-        src_ref=ORX.at[pl.ds(0, ND - 1)],
-        dst_ref=ORX.at[pl.ds(0, ND - 1)],
-        send_sem=o_send,
-        recv_sem=o_recv,
-        device_id=(i, right_j),
-        device_id_type=MESH,
-    )
-    back.wait_recv()
+
+        def start():
+            pltpu.make_async_remote_copy(
+                src_ref=OM.at[b],
+                dst_ref=ORX.at[slot],
+                send_sem=o_send,
+                recv_sem=o_recv,
+                device_id=(block, b),
+                device_id_type=MESH,
+            ).start()
+
+        if d == 0:
+            pl.when(jnp.logical_not(home))(start)
+        else:
+            start()
+
+    @pl.when(home)
+    def _():
+        ORX[slot] = OM[j]
+
+    one_less(home, ORX, ND, o_send, o_recv, wait_recv)
     low = iota((8, 128), 0) < 4
     for which, out in ((0, x_out), (1, r_out)):
         groups = jnp.concatenate([ORX[2 * t + which, g] for t in range(TR // 8) for g in range(2)], 0)
@@ -599,36 +645,19 @@
             out[8 * t : 8 * t + 8, 0:128] = jnp.where(low, a, pltpu.roll(b, 4, 0))
             out[8 * t : 8 * t + 8, 128:256] = jnp.where(low, pltpu.roll(a, 4, 0), b)
 
-    back.wait_send()
+    one_less(home, ORX, ND, o_send, o_recv, wait_send)
     for c in halos:
         c.wait_send()
     for f in (0, 1):
-        pltpu.make_async_remote_copy(
-            src_ref=rx.at[f, pl.ds(0, ND - 1)],
-            dst_ref=rx.at[f, pl.ds(0, ND - 1)],
-            send_sem=rx_send.at[f],
-            recv_sem=rx_recv.at[f],
-            device_id=(i, right_j),
-            device_id_type=MESH,
-        ).wait_send()
-        pltpu.make_async_remote_copy(
-            src_ref=rxv.at[f, pl.ds(0, 4)],
-            dst_ref=rxv.at[f, pl.ds(0, 4)],
-            send_sem=rxv_send.at[f],
-            recv_sem=rxv_recv.at[f],
-            device_id=(i, right_j),
-            device_id_type=MESH,
-        ).wait_send()
+        one_less(home, rx.at[f], ND, rx_send.at[f], rx_recv.at[f], wait_send)
+        bytes_of(S.at[f, pl.ds(0, 384)], s_send.at[f], s_recv.at[f]).wait_send()
+        one_less(
+            below_self | above_self, rxv.at[f], 2, rxv_send.at[f], rxv_recv.at[f], wait_send
+        )
     for slot in range(2 if mode == "fast" else ITERS):
-        for half, dst in ((0, g1), (1, g2)):
-            pltpu.make_async_remote_copy(
-                src_ref=dst.at[slot, pl.ds(0, ND - 1)],
-                dst_ref=dst.at[slot, pl.ds(0, ND - 1)],
-                send_sem=g_send.at[2 * slot + half],
-                recv_sem=g_recv.at[2 * slot + half],
-                device_id=(i, right_j),
-                device_id_type=MESH,
-            ).wait_send()
+        first = slot == 0 and mode == "fast"
+        group_bytes(g1.at[slot], 2 * slot, ND).wait_send()
+        group_bytes(g2.at[slot], 2 * slot + 1, ND if first else ND // 2).wait_send()
 
 
 def run(mode, events, entry_week, exit_week, log_offset, frailty, kappa_sq, log_rate, shape_rate):
@@ -640,12 +669,17 @@
         out_shape=(
             jax.ShapeDtypeStruct((TR, TC), f32),
             jax.ShapeDtypeStruct((TR, TC), f32),
-            jax.ShapeDtypeStruct((8, 128), f32),
+            jax.ShapeDtypeStruct((1,), jnp.int32),
         ),
-        in_specs=[pl.BlockSpec(memory_space=pltpu.SMEM)] * 2
-        + [pl.BlockSpec(memory_space=pl.ANY)] * 6,
-        out_specs=(pl.BlockSpec(memory_space=pltpu.VMEM),) * 3,
+        in_specs=[pl.BlockSpec(memory_space=pltpu.HBM)] * 8,
+        out_specs=(
+            pl.BlockSpec(memory_space=pltpu.VMEM),
+            pl.BlockSpec(memory_space=pltpu.VMEM),
+            pl.BlockSpec(memory_space=pltpu.SMEM),
+        ),
         scratch_shapes=[
+            pltpu.SMEM((1,), f32),
+            pltpu.SMEM((1,), f32),
             vm(events.shape, jnp.int32),
             vm((TR, TC), jnp.int32),
             vm((TR, TC), jnp.int32),
@@ -656,9 +690,9 @@
             vm((2, 8, TC), f32),
             vm((2, TR, 128), f32),
             vm((2, GR, 8, 128), f32),
-            vm((2, ND, 6, 8, 128), f32),
+            vm((2, ND, 3, 8, 128), f32),
             vm((2, ND, 2, 8, 128), f32),
-            vm((768, 128), f32),
+            vm((2, 768, 128), f32),
             vm((K, 24, 128), f32),
             vm((K, 24, 128), f32),
             vm((K, 24, 128), f32),
@@ -678,7 +712,7 @@
             vm((256, 128), f32),
             vm((ND, 2, 8, 128), f32),
             vm((ND, 2, 8, 128), f32),
-            dma((5 + EV_PARTS,)),
+            dma((7 + EV_PARTS,)),
             dma((4,)),
             dma((4,)),
             dma((2,)),
@@ -689,6 +723,8 @@
             dma((2 * slots,)),
             dma,
             dma,
+            dma((2,)),
+            dma((2,)),
         ],
         compiler_params=pltpu.CompilerParams(
             collective_id=0 if mode == "fast" else 1,
@@ -702,7 +738,7 @@
 def per_device(*args):
     step, residual, flag = run("fast", *args)
     return lax.cond(
-        flag[0, 0] > PIVOT_MIN,
+        flag[0] > 0,
         lambda: (step, residual),
         lambda: tuple(run("cg", *args)[:2]),
     )

time: 59.2 us -> 53.6 us (0.905)
  Pallas kernels: 54.1 us -> 49 us
    pallas_call x1, Pallas kernels: 54.1 us -> 49 us  [run(): pl.pallas_call(functools.partial(kernel, mode), out_shape=(jax.ShapeDtype...]
where the time goes in v1:
time: 53.6 us; the launch traced here: 53.5 us
  Pallas kernels  49 us (91%)
  between operations  3.17 us (6%)
  local copies, waits for them, and re-layouts  1.29 us (2%)
    pallas_call x1, Pallas kernels, run(): pl.pallas_call(functools.partial(kernel, mode), out_shape=(jax.ShapeDtype...  49 us
    unnamed x14, local copies, waits for them, and re-layouts  1.29 us

profile of v1, /device:TPU:1, one launch (start us, length us, event | category | flops | bytes accessed | tf_op | source)
XLA Modules:
  0.0 53.5 jit_solution(12358294401049321082)
XLA Ops:
  0.6 0.0 copy-start.5
  0.6 0.0 copy-start.4
  0.7 0.0 copy-start.3
  0.7 0.0 copy-start.2
  0.7 0.0 copy-start.1
  0.7 0.0 copy-start
  2.5 49.0 %newton_fast.1 = (f32[64,256]{1,0:T(8,128)S(1)}, f32[64,256]{1,0:T(8,128)S(1)}, s32[1]{0:T(128)}) custom-call(f32[1]{0:T(128)S(6)} %copy.16.lr_hbm, f32[1]{0:T(128)S(6)} %copy.17.sr_hbm, s32[52,64,256]{2,1,0:T(8,128)} %ev_hbm.1, s32[64,256]{1,0:T(8,128)} %en_hbm.1, s32[64,256]{1,0:T(8,128)} %ex_hbm.1, f32[64,256]{1,0:T(8,128)} %lo_hbm.1, f32[64,256]{1,0:T(8,128)} %fr_hbm.1, ...), custom_call_target="tpu_custom_call" | custom-call | tf_op jit(solution)/shard_map/newton_fast/pallas_call | solution.py:667
  52.2 0.0 copy-done.5
  52.2 0.0 copy-done.4
  52.2 0.0 copy-done.3
  52.2 0.0 copy-done.2
  52.2 0.0 copy-done.1
  52.2 0.0 copy-done
  52.2 0.6 %copy.18 = f32[64,256]{1,0:T(8,128)} copy(f32[64,256]{1,0:T(8,128)S(1)} %get-tuple-element.44) | data formatting | bytes 131072
  52.9 0.6 %copy.19 = f32[64,256]{1,0:T(8,128)} copy(f32[64,256]{1,0:T(8,128)S(1)} %get-tuple-element.45) | data formatting | bytes 131072
  (1 shorter events, 0.0 us)
Async XLA Ops:
  0.6 51.5 %copy-start.5 = (f32[64,256]{1,0:T(8,128)S(1)}, f32[64,256]{1,0:T(8,128)}, u32[]{:S(2)}) copy-start(f32[64,256]{1,0:T(8,128)} %ka_hbm.1) | copy-start | bytes 196612
  0.6 51.5 %copy-start.4 = (f32[64,256]{1,0:T(8,128)S(1)}, f32[64,256]{1,0:T(8,128)}, u32[]{:S(2)}) copy-start(f32[64,256]{1,0:T(8,128)} %fr_hbm.1) | copy-start | bytes 196612
  0.7 51.5 %copy-start.3 = (f32[64,256]{1,0:T(8,128)S(1)}, f32[64,256]{1,0:T(8,128)}, u32[]{:S(2)}) copy-start(f32[64,256]{1,0:T(8,128)} %lo_hbm.1) | copy-start | bytes 196612
  0.7 51.5 %copy-start.2 = (s32[64,256]{1,0:T(8,128)S(1)}, s32[64,256]{1,0:T(8,128)}, u32[]{:S(2)}) copy-start(s32[64,256]{1,0:T(8,128)} %ex_hbm.1) | copy-start | bytes 196612
  0.7 51.5 %copy-start.1 = (s32[64,256]{1,0:T(8,128)S(1)}, s32[64,256]{1,0:T(8,128)}, u32[]{:S(2)}) copy-start(s32[64,256]{1,0:T(8,128)} %en_hbm.1) | copy-start | bytes 196612
  0.7 51.5 %copy-start = (s32[52,64,256]{2,1,0:T(8,128)S(1)}, s32[52,64,256]{2,1,0:T(8,128)}, u32[]{:S(2)}) copy-start(s32[52,64,256]{2,1,0:T(8,128)} %ev_hbm.1) | copy-start | bytes 10223620

commit v2 on v1

--- a/solution.py
+++ b/solution.py
@@ -17,11 +17,27 @@
 GR = 20
 EV_PARTS = 4
 PIVOT_MIN = 2e-3
+W = 2
 f32 = jnp.float32
 
 
 def iota(shape, dim):
     return lax.broadcasted_iota(jnp.int32, shape, dim)
+
+
+def turn(x, by):
+    by = by % 128
+    return pltpu.roll(x, by, 1) if by else x
+
+
+def compose(later, earlier):
+    out = {}
+    for o, x in later.items():
+        for q, y in earlier.items():
+            term = x * turn(y, o)
+            at = (o + q) % 128
+            out[at] = out[at] + term if at in out else term
+    return out
 
 
 def seg_transpose(x):
@@ -69,6 +85,7 @@
     ka,
     e_ref,
     hv_rx,
+    hh_tx,
     hh_rx,
     U,
     rx,
@@ -176,6 +193,9 @@
     for c in loads:
         c.wait()
 
+    flipped = jnp.concatenate([fr[:, 128:256], fr[:, 0:128]], 0).T
+    hh_tx[0] = flipped[120:128]
+    hh_tx[1] = flipped[0:8]
     rate = jnp.full((1, TC), sr_ref[0], f32)
     scale = jnp.exp(jnp.full((1, TC), lr_ref[0], f32)) / rate
     slope = rate / float(ev.shape[0])
@@ -193,7 +213,8 @@
     ).reshape(TR // 4, 8, 128)
     part = diag - 2.0
     part = part[:, 0:128] + part[:, 128:256]
-    m1[0] = jnp.sum(part.reshape(8, 8, 128), axis=0)
+    part = jnp.sum(part, axis=0, keepdims=True)
+    m1[0] = jnp.where(iota((W, 128), 0) == 0, part, 0.0)
 
     def send_field(f):
         for q in (0, 1):
@@ -302,8 +323,8 @@
             (
                 (fr.at[pl.ds(TR - 8, 8)], hv_rx.at[0], (down_i, j)),
                 (fr.at[pl.ds(0, 8)], hv_rx.at[1], (up_i, j)),
-                (fr.at[:, pl.ds(128, 128)], hh_rx.at[0], (i, right_j)),
-                (fr.at[:, pl.ds(0, 128)], hh_rx.at[1], (i, left_j)),
+                (hh_tx.at[0], hh_rx.at[0], (i, right_j)),
+                (hh_tx.at[1], hh_rx.at[1], (i, left_j)),
             )
         )
     ]
@@ -332,18 +353,20 @@
     lane = iota((TR, 128), 1)
     has_up, has_down = jnp.where(i > 0, 1.0, 0.0), jnp.where(i < ND - 1, 1.0, 0.0)
     has_left, has_right = jnp.where(j > 0, 1.0, 0.0), jnp.where(j < ND - 1, 1.0, 0.0)
+    lane1 = iota((1, 128), 1)
+    edges = jnp.where(lane1 < TR, hh_rx[0, 7:8] * has_left, hh_rx[1, 0:1] * has_right)
+    edges = jnp.broadcast_to(edges, (128, 128)).T
     halves = []
     for h in (0, 1):
         cols = slice(128 * h, 128 * h + 128)
         here = fr[:, cols]
         above = jnp.where(row == 0, hv_rx[0, 7:8, cols] * has_up, pltpu.roll(here, 1, 0))
         below = jnp.where(row == TR - 1, hv_rx[1, 0:1, cols] * has_down, pltpu.roll(here, TR - 1, 0))
-        if h == 0:
-            beside_l, beside_r = hh_rx[0] * has_left, fr[:, 128:256]
-        else:
-            beside_l, beside_r = fr[:, 0:128], hh_rx[1] * has_right
-        west = jnp.where(lane == 0, pltpu.roll(beside_l, 1, 1), pltpu.roll(here, 1, 1))
-        east = jnp.where(lane == 127, pltpu.roll(beside_r, 127, 1), pltpu.roll(here, 127, 1))
+        there = fr[:, 128 - 128 * h : 256 - 128 * h]
+        west_in = edges[0:TR] if h == 0 else pltpu.roll(there, 1, 1)
+        east_in = pltpu.roll(there, 127, 1) if h == 0 else edges[TR : 2 * TR]
+        west = jnp.where(lane == 0, west_in, pltpu.roll(here, 1, 1))
+        east = jnp.where(lane == 127, east_in, pltpu.roll(here, 127, 1))
         total = e_ref[:, cols] + TAU * ((below + above) + (east + west))
         halves.append(total * (1.0 / TAU))
     U[1, 2 : GR - 2] = to_groups(lambda t, h: halves[h][8 * t : 8 * t + 8, :]).reshape(TR // 4, 8, 128)
@@ -430,40 +453,49 @@
     pivot = 1.0 / (Y[K - 1] - p - after(w_u))
     lo_c = jnp.where(lanes24 == 0, 0.0, last_u) * pivot
     hi_c = after(last_u) * pivot
-    pcr[0, 0] = pivot
+    levels = [{0: pivot}]
     for n in range(7):
         s = 1 << n
-        d = 1.0 / (1.0 - lo_c * pltpu.roll(hi_c, s, 1) - hi_c * pltpu.roll(lo_c, 128 - s, 1))
+        d = 1.0 / (1.0 - lo_c * turn(hi_c, s) - hi_c * turn(lo_c, -s))
         a, b = d * lo_c, d * hi_c
-        pcr[n + 1, 0] = d
-        pcr[n + 1, 1] = a
-        pcr[n + 1, 2] = b
-        lo_c = a * pltpu.roll(lo_c, s, 1)
-        hi_c = b * pltpu.roll(hi_c, 128 - s, 1)
+        levels.append({0: d, s: a, 128 - s: b} if n < 6 else {0: d, s: a + b})
+        lo_c = a * turn(lo_c, s)
+        hi_c = b * turn(hi_c, -s)
+    steps = (
+        compose(levels[3], compose(levels[2], compose(levels[1], levels[0]))),
+        compose(levels[7], compose(levels[6], compose(levels[5], levels[4]))),
+    )
+    offsets = [sorted(step) for step in steps]
+    place = {}
+    for n, step in enumerate(steps):
+        for o in offsets[n]:
+            place[n, o] = len(place)
+            pcr[place[n, o]] = step[o]
 
     to_lines(1, RHS, 0.0)
 
     def solve(put):
-        r = RHS[0]
-        f = inv[0] * r
-        ends = u[0] * r
-        Y[0] = f
+        first = [u[k] * RHS[k] for k in range(4)]
+        last = [v[k] * RHS[k] for k in range(4)]
+        for k in range(4, K - 1):
+            first[k % 4] = first[k % 4] + u[k] * RHS[k]
+            last[k % 4] = last[k % 4] + v[k] * RHS[k]
+        x = after((first[0] + first[1]) + (first[2] + first[3]))
+        x = x + ((last[0] + last[1]) + (last[2] + last[3])) + RHS[K - 1]
+        f = inv[0] * RHS[0]
+        fs = [f]
         for k in range(1, K - 1):
-            r = RHS[k]
-            ends = ends + u[k] * r
-            f = inv[k] * (r + f)
+            f = inv[k] * (RHS[k] + f)
             Y[k] = f
-        x = pcr[0, 0] * (RHS[K - 1] + f + after(ends))
-        for n in range(7):
-            s = 1 << n
-            x = (
-                pcr[n + 1, 0] * x
-                + pcr[n + 1, 1] * pltpu.roll(x, s, 1)
-                + pcr[n + 1, 2] * pltpu.roll(x, 128 - s, 1)
-            )
-        for k in range(K - 3, -1, -1):
+        for n in range(2):
+            terms = [pcr[place[n, o]] * turn(x, o) for o in offsets[n]]
+            while len(terms) > 1:
+                terms = [sum(terms[t : t + 2][1:], terms[t]) for t in range(0, len(terms), 2)]
+            x = terms[0]
+        for k in range(K - 3, 0, -1):
             f = Y[k] + inv[k] * f
             Y[k] = f
+        Y[0] = fs[0] + inv[0] * f
         prev = before(x)
         put(K - 1, x)
         for k in range(K - 2, -1, -1):
@@ -520,7 +552,8 @@
             return 0
 
         lax.fori_loop(0, ITERS, basis, 0)
-        m1[1] = jnp.sum(GM[...].T.reshape(16, 8, 128), axis=0)
+        part = jnp.sum(GM[...].T, axis=0, keepdims=True)
+        m1[1] = jnp.where(iota((W, 128), 0) == 0, part, 0.0)
         total = exchange(1)
         flat = jnp.sum(total, axis=0, keepdims=True)
         mat = pltpu.roll(jnp.broadcast_to(flat, (8, 128)), 0, 1, stride=8, stride_axis=0)
@@ -579,7 +612,7 @@
             solve(put)
             gam = jnp.sum(acc[0] + acc[1], axis=0, keepdims=True)
             mu = jnp.sum(acc[2] + acc[3], axis=0, keepdims=True)
-            m1[it] = jnp.where(sub8 == 0, gam, jnp.where(sub8 == 1, mu, 0.0))
+            m1[it] = jnp.where(iota((W, 128), 0) == 0, gam, mu)
             total = jnp.sum(exchange(it), axis=1, keepdims=True)
             gamma = total[0:1]
             mu = total[1:2]
@@ -688,7 +721,8 @@
             vm((TR, TC), f32),
             vm((TR, TC), f32),
             vm((2, 8, TC), f32),
-            vm((2, TR, 128), f32),
+            vm((2, 8, 128), f32),
+            vm((2, 8, 128), f32),
             vm((2, GR, 8, 128), f32),
             vm((2, ND, 3, 8, 128), f32),
             vm((2, ND, 2, 8, 128), f32),
@@ -696,7 +730,7 @@
             vm((K, 24, 128), f32),
             vm((K, 24, 128), f32),
             vm((K, 24, 128), f32),
-            vm((8, 3, 24, 128), f32),
+            vm((31, 24, 128), f32),
             vm((K, 24, 128), f32),
             vm((K, 24, 128), f32),
             vm((ITERS + 2, K, 24, 128), f32),
@@ -705,10 +739,10 @@
             vm((24, 128), f32),
             vm((24, 128), f32),
             vm((128, 128), f32),
-            vm((slots, 8, 128), f32),
-            vm((slots, 8, 128), f32),
-            vm((slots, ND, 8, 128), f32),
-            vm((slots, ND, 8, 128), f32),
+            vm((slots, W, 128), f32),
+            vm((slots, W, 128), f32),
+            vm((slots, ND, W, 128), f32),
+            vm((slots, ND, W, 128), f32),
             vm((256, 128), f32),
             vm((ND, 2, 8, 128), f32),
             vm((ND, 2, 8, 128), f32),

time: 53.6 us -> 49.8 us (0.929)
  Pallas kernels: 49 us -> 45.3 us
    pallas_call x1, Pallas kernels: 49 us -> 45.3 us  [run(): pl.pallas_call(functools.partial(kernel, mode), out_shape=(jax.ShapeDtype...]
where the time goes in v2:
time: 49.8 us; the launch traced here: 49.7 us
  Pallas kernels  45.3 us (91%)
  between operations  3.17 us (6%)
  local copies, waits for them, and re-layouts  1.29 us (3%)
    pallas_call x1, Pallas kernels, run(): pl.pallas_call(functools.partial(kernel, mode), out_shape=(jax.ShapeDtype...  45.3 us
    unnamed x14, local copies, waits for them, and re-layouts  1.29 us

profile of v2, /device:TPU:1, one launch (start us, length us, event | category | flops | bytes accessed | tf_op | source)
XLA Modules:
  0.0 49.7 jit_solution(4366976101819401782)
XLA Ops:
  0.6 0.0 copy-start.5
  0.6 0.0 copy-start.4
  0.7 0.0 copy-start.3
  0.7 0.0 copy-start.2
  0.7 0.0 copy-start.1
  0.7 0.0 copy-start
  2.5 45.3 %newton_fast.1 = (f32[64,256]{1,0:T(8,128)S(1)}, f32[64,256]{1,0:T(8,128)S(1)}, s32[1]{0:T(128)}) custom-call(f32[1]{0:T(128)S(6)} %copy.16.lr_hbm, f32[1]{0:T(128)S(6)} %copy.17.sr_hbm, s32[52,64,256]{2,1,0:T(8,128)} %ev_hbm.1, s32[64,256]{1,0:T(8,128)} %en_hbm.1, s32[64,256]{1,0:T(8,128)} %ex_hbm.1, f32[64,256]{1,0:T(8,128)} %lo_hbm.1, f32[64,256]{1,0:T(8,128)} %fr_hbm.1, ...), custom_call_target="tpu_custom_call" | custom-call | tf_op jit(solution)/shard_map/newton_fast/pallas_call | solution.py:700
  48.4 0.0 copy-done.5
  48.4 0.0 copy-done.4
  48.4 0.0 copy-done.3
  48.4 0.0 copy-done.2
  48.4 0.0 copy-done.1
  48.4 0.0 copy-done
  48.5 0.6 %copy.18 = f32[64,256]{1,0:T(8,128)} copy(f32[64,256]{1,0:T(8,128)S(1)} %get-tuple-element.44) | data formatting | bytes 131072
  49.1 0.6 %copy.19 = f32[64,256]{1,0:T(8,128)} copy(f32[64,256]{1,0:T(8,128)S(1)} %get-tuple-element.45) | data formatting | bytes 131072
  (1 shorter events, 0.0 us)
Async XLA Ops:
  0.6 47.8 %copy-start.5 = (f32[64,256]{1,0:T(8,128)S(1)}, f32[64,256]{1,0:T(8,128)}, u32[]{:S(2)}) copy-start(f32[64,256]{1,0:T(8,128)} %ka_hbm.1) | copy-start | bytes 196612
  0.6 47.8 %copy-start.4 = (f32[64,256]{1,0:T(8,128)S(1)}, f32[64,256]{1,0:T(8,128)}, u32[]{:S(2)}) copy-start(f32[64,256]{1,0:T(8,128)} %fr_hbm.1) | copy-start | bytes 196612
  0.7 47.8 %copy-start.3 = (f32[64,256]{1,0:T(8,128)S(1)}, f32[64,256]{1,0:T(8,128)}, u32[]{:S(2)}) copy-start(f32[64,256]{1,0:T(8,128)} %lo_hbm.1) | copy-start | bytes 196612
  0.7 47.8 %copy-start.2 = (s32[64,256]{1,0:T(8,128)S(1)}, s32[64,256]{1,0:T(8,128)}, u32[]{:S(2)}) copy-start(s32[64,256]{1,0:T(8,128)} %ex_hbm.1) | copy-start | bytes 196612
  0.7 47.8 %copy-start.1 = (s32[64,256]{1,0:T(8,128)S(1)}, s32[64,256]{1,0:T(8,128)}, u32[]{:S(2)}) copy-start(s32[64,256]{1,0:T(8,128)} %en_hbm.1) | copy-start | bytes 196612
  0.7 47.8 %copy-start = (s32[52,64,256]{2,1,0:T(8,128)S(1)}, s32[52,64,256]{2,1,0:T(8,128)}, u32[]{:S(2)}) copy-start(s32[52,64,256]{2,1,0:T(8,128)} %ev_hbm.1) | copy-start | bytes 10223620

commit v3 on v2

--- a/solution.py
+++ b/solution.py
@@ -72,8 +72,7 @@
     lo_hbm,
     fr_hbm,
     ka_hbm,
-    x_out,
-    r_out,
+    both_out,
     flag_out,
     lr_ref,
     sr_ref,
@@ -330,9 +329,9 @@
     ]
     for c in halos:
         c.start()
+    send_field(0)
     if mode == "fast":
         group_sends(m1.at[0], g1.at[0], 0, "row")
-    send_field(0)
 
     en_v, ex_v = en[...], ex[...]
     count = jnp.zeros((TR, TC), jnp.int32)
@@ -431,12 +430,12 @@
     def before(x):
         return jnp.where(lanes24 == 0, 0.0, pltpu.roll(x, 1, 1))
 
-    p = 1.0 / Y[0]
+    p = MK[...] / Y[0]
     inv[0] = p
     prod = p
     u[0] = prod
     for k in range(1, K - 1):
-        p = 1.0 / (Y[k] - p)
+        p = MK[...] / (Y[k] - p)
         inv[k] = p
         prod = prod * p
         u[k] = prod
@@ -450,7 +449,7 @@
         v[k] = q
         w_u = u[k] + p_k * w_u
         u[k] = w_u
-    pivot = 1.0 / (Y[K - 1] - p - after(w_u))
+    pivot = MK[...] / (Y[K - 1] - p - after(w_u))
     lo_c = jnp.where(lanes24 == 0, 0.0, last_u) * pivot
     hi_c = after(last_u) * pivot
     levels = [{0: pivot}]
@@ -502,7 +501,7 @@
             put(k, Y[k] + (u[k] * prev + v[k] * x))
 
     def across(z):
-        return MK[...] * (2.0 * z - (pltpu.roll(z, 1, 0) + pltpu.roll(z, 23, 0)))
+        return 2.0 * z - (pltpu.roll(z, 1, 0) + pltpu.roll(z, 23, 0))
 
     own = slice(8, 16)
     sub8 = iota((8, 128), 0)
@@ -669,14 +668,14 @@
 
     one_less(home, ORX, ND, o_send, o_recv, wait_recv)
     low = iota((8, 128), 0) < 4
-    for which, out in ((0, x_out), (1, r_out)):
+    for which in (0, 1):
         groups = jnp.concatenate([ORX[2 * t + which, g] for t in range(TR // 8) for g in range(2)], 0)
         groups = seg_transpose(groups)
         for t in range(TR // 8):
             a = groups[16 * t : 16 * t + 8]
             b = groups[16 * t + 8 : 16 * t + 16]
-            out[8 * t : 8 * t + 8, 0:128] = jnp.where(low, a, pltpu.roll(b, 4, 0))
-            out[8 * t : 8 * t + 8, 128:256] = jnp.where(low, pltpu.roll(a, 4, 0), b)
+            both_out[which, 8 * t : 8 * t + 8, 0:128] = jnp.where(low, a, pltpu.roll(b, 4, 0))
+            both_out[which, 8 * t : 8 * t + 8, 128:256] = jnp.where(low, pltpu.roll(a, 4, 0), b)
 
     one_less(home, ORX, ND, o_send, o_recv, wait_send)
     for c in halos:
@@ -700,13 +699,11 @@
     return pl.pallas_call(
         functools.partial(kernel, mode),
         out_shape=(
-            jax.ShapeDtypeStruct((TR, TC), f32),
-            jax.ShapeDtypeStruct((TR, TC), f32),
+            jax.ShapeDtypeStruct((2, TR, TC), f32),
             jax.ShapeDtypeStruct((1,), jnp.int32),
         ),
         in_specs=[pl.BlockSpec(memory_space=pltpu.HBM)] * 8,
         out_specs=(
-            pl.BlockSpec(memory_space=pltpu.VMEM),
             pl.BlockSpec(memory_space=pltpu.VMEM),
             pl.BlockSpec(memory_space=pltpu.SMEM),
         ),
@@ -726,7 +723,7 @@
             vm((2, GR, 8, 128), f32),
             vm((2, ND, 3, 8, 128), f32),
             vm((2, ND, 2, 8, 128), f32),
-            vm((2, 768, 128), f32),
+            vm((2, 800, 128), f32),
             vm((K, 24, 128), f32),
             vm((K, 24, 128), f32),
             vm((K, 24, 128), f32),
@@ -743,7 +740,7 @@
             vm((slots, W, 128), f32),
             vm((slots, ND, W, 128), f32),
             vm((slots, ND, W, 128), f32),
-            vm((256, 128), f32),
+            vm((288, 128), f32),
             vm((ND, 2, 8, 128), f32),
             vm((ND, 2, 8, 128), f32),
             dma((7 + EV_PARTS,)),
@@ -770,12 +767,9 @@
 
 
 def per_device(*args):
-    step, residual, flag = run("fast", *args)
-    return lax.cond(
-        flag[0] > 0,
-        lambda: (step, residual),
-        lambda: tuple(run("cg", *args)[:2]),
-    )
+    both, flag = run("fast", *args)
+    both = lax.cond(flag[0] > 0, lambda: both, lambda: run("cg", *args)[0])
+    return both[0], both[1]
 
 
 def solution(mesh):

time: 49.8 us -> 49.1 us (0.986)
  local copies, waits for them, and re-layouts: 1.29 us -> 0.68 us
    unnamed x14 -> x12, local copies, waits for them, and re-layouts: 1.29 us -> 0.03 us
    squeeze x0 -> x1, local copies, waits for them, and re-layouts: none -> 0.66 us  [per_device(): return (both[0], both[1])]
where the time goes in v3:
time: 49.1 us; the launch traced here: 49 us
  Pallas kernels  45.1 us (92%)
  between operations  3.17 us (6%)
  local copies, waits for them, and re-layouts  0.68 us (1%)
    pallas_call x1, Pallas kernels, run(): pl.pallas_call(functools.partial(kernel, mode), out_shape=(jax.ShapeDtype...  45.1 us

profile of v3, /device:TPU:1, one launch (start us, length us, event | category | flops | bytes accessed | tf_op | source)
XLA Modules:
  0.0 49.0 jit_solution(13685424370286278772)
XLA Ops:
  0.6 0.0 copy-start.5
  0.6 0.0 copy-start.4
  0.7 0.0 copy-start.3
  0.7 0.0 copy-start.2
  0.7 0.0 copy-start.1
  0.7 0.0 copy-start
  2.5 45.1 %newton_fast.1 = (f32[2,64,256]{2,1,0:T(8,128)S(1)}, s32[1]{0:T(128)}) custom-call(f32[1]{0:T(128)S(6)} %copy.12.lr_hbm, f32[1]{0:T(128)S(6)} %copy.13.sr_hbm, s32[52,64,256]{2,1,0:T(8,128)} %ev_hbm.1, s32[64,256]{1,0:T(8,128)} %en_hbm.1, s32[64,256]{1,0:T(8,128)} %ex_hbm.1, f32[64,256]{1,0:T(8,128)} %lo_hbm.1, f32[64,256]{1,0:T(8,128)} %fr_hbm.1, ...), custom_call_target="tpu_custom_call" | custom-call | tf_op jit(solution)/shard_map/newton_fast/pallas_call | solution.py:699
  48.2 0.0 copy-done.5
  48.2 0.0 copy-done.4
  48.3 0.0 copy-done.3
  48.3 0.0 copy-done.2
  48.3 0.0 copy-done.1
  48.3 0.0 copy-done
  48.3 0.7 %slice_bitcast_fusion = (f32[64,256]{1,0:T(8,128)}, f32[64,256]{1,0:T(8,128)}) fusion(f32[2,64,256]{2,1,0:T(8,128)S(1)} %get-tuple-element.37), kind=kLoop, calls=%fused_computation | loop fusion | bytes 262144 | tf_op jit(solution)/shard_map/squeeze | solution.py:772
  (1 shorter events, 0.0 us)
Async XLA Ops:
  0.6 47.6 %copy-start.5 = (f32[64,256]{1,0:T(8,128)S(1)}, f32[64,256]{1,0:T(8,128)}, u32[]{:S(2)}) copy-start(f32[64,256]{1,0:T(8,128)} %ka_hbm.1) | copy-start | bytes 196612
  0.6 47.6 %copy-start.4 = (f32[64,256]{1,0:T(8,128)S(1)}, f32[64,256]{1,0:T(8,128)}, u32[]{:S(2)}) copy-start(f32[64,256]{1,0:T(8,128)} %fr_hbm.1) | copy-start | bytes 196612
  0.7 47.6 %copy-start.3 = (f32[64,256]{1,0:T(8,128)S(1)}, f32[64,256]{1,0:T(8,128)}, u32[]{:S(2)}) copy-start(f32[64,256]{1,0:T(8,128)} %lo_hbm.1) | copy-start | bytes 196612
  0.7 47.6 %copy-start.2 = (s32[64,256]{1,0:T(8,128)S(1)}, s32[64,256]{1,0:T(8,128)}, u32[]{:S(2)}) copy-start(s32[64,256]{1,0:T(8,128)} %ex_hbm.1) | copy-start | bytes 196612
  0.7 47.6 %copy-start.1 = (s32[64,256]{1,0:T(8,128)S(1)}, s32[64,256]{1,0:T(8,128)}, u32[]{:S(2)}) copy-start(s32[64,256]{1,0:T(8,128)} %en_hbm.1) | copy-start | bytes 196612
  0.7 47.6 %copy-start = (s32[52,64,256]{2,1,0:T(8,128)S(1)}, s32[52,64,256]{2,1,0:T(8,128)}, u32[]{:S(2)}) copy-start(s32[52,64,256]{2,1,0:T(8,128)} %ev_hbm.1) | copy-start | bytes 10223620

commit v4 on v3

--- a/solution.py
+++ b/solution.py
@@ -133,39 +133,6 @@
     up_i, down_i = (i + ND - 1) % ND, (i + 1) % ND
     left_j, right_j = (j + ND - 1) % ND, (j + 1) % ND
 
-    barrier = pltpu.get_barrier_semaphore()
-
-    def hello(a, b):
-        pl.semaphore_signal(barrier, inc=1, device_id=(a, b), device_id_type=MESH)
-
-    for d in range(1, ND):
-        hello(i, (j + d) % ND)
-    for d in range(1, ND):
-        hello((i + d) % ND, j)
-    for d in range(8):
-        hello(other, 8 * core + d)
-
-    @pl.when(jnp.logical_not(home))
-    def _():
-        for b in range(ND):
-            hello(other, b)
-
-    ghost_first = (core == 0) & (m == 0)
-    ghost_last = (core == 1) & (m == 7)
-    ghost_from = (block + jnp.where(core == 0, ND - 1, 1)) % ND
-    below_dev = (2 * (down_i // 2), 8 * (down_i % 2))
-    above_dev = (2 * (up_i // 2) + 1, 8 * (up_i % 2) + 7)
-    below_self = (below_dev[0] == i) & (below_dev[1] == j)
-    above_self = (above_dev[0] == i) & (above_dev[1] == j)
-
-    @pl.when(ghost_first | ghost_last)
-    def _():
-        for b in range(ND):
-
-            @pl.when(jnp.logical_not((ghost_from == i) & (j == b)))
-            def _():
-                hello(ghost_from, b)
-
     loads = [
         pltpu.make_async_copy(src, dst, in_sem.at[n])
         for n, (src, dst) in enumerate(
@@ -180,6 +147,42 @@
             )
         )
     ]
+    for c in loads:
+        c.start()
+
+    barrier = pltpu.get_barrier_semaphore()
+
+    def hello(a, b):
+        pl.semaphore_signal(barrier, inc=1, device_id=(a, b), device_id_type=MESH)
+
+    for d in range(1, ND):
+        hello(i, (j + d) % ND)
+    for d in range(1, ND):
+        hello((i + d) % ND, j)
+    for d in range(8):
+        hello(other, 8 * core + d)
+
+    @pl.when(jnp.logical_not(home))
+    def _():
+        for b in range(ND):
+            hello(other, b)
+
+    ghost_first = (core == 0) & (m == 0)
+    ghost_last = (core == 1) & (m == 7)
+    ghost_from = (block + jnp.where(core == 0, ND - 1, 1)) % ND
+    below_dev = (2 * (down_i // 2), 8 * (down_i % 2))
+    above_dev = (2 * (up_i // 2) + 1, 8 * (up_i % 2) + 7)
+    below_self = (below_dev[0] == i) & (below_dev[1] == j)
+    above_self = (above_dev[0] == i) & (above_dev[1] == j)
+
+    @pl.when(ghost_first | ghost_last)
+    def _():
+        for b in range(ND):
+
+            @pl.when(jnp.logical_not((ghost_from == i) & (j == b)))
+            def _():
+                hello(ghost_from, b)
+
     weeks = ev.shape[0] // EV_PARTS
     ev_loads = [
         pltpu.make_async_copy(
@@ -187,7 +190,7 @@
         )
         for n in range(EV_PARTS)
     ]
-    for c in loads + ev_loads:
+    for c in ev_loads:
         c.start()
     for c in loads:
         c.wait()

time: 49.1 us -> 49.1 us (level)
  no operation moved by 1% of the time
where the time goes in v4:
time: 49.1 us; the launch traced here: 49 us
  Pallas kernels  45.1 us (92%)
  between operations  3.17 us (6%)
  local copies, waits for them, and re-layouts  0.68 us (1%)
    pallas_call x1, Pallas kernels, run(): pl.pallas_call(functools.partial(kernel, mode), out_shape=(jax.ShapeDtype...  45.1 us

profile of v4, /device:TPU:1, one launch (start us, length us, event | category | flops | bytes accessed | tf_op | source)
XLA Modules:
  0.0 49.0 jit_solution(8747336053817535800)
XLA Ops:
  0.6 0.0 copy-start.5
  0.6 0.0 copy-start.4
  0.7 0.0 copy-start.3
  0.7 0.0 copy-start.2
  0.7 0.0 copy-start.1
  0.7 0.0 copy-start
  2.5 45.1 %newton_fast.1 = (f32[2,64,256]{2,1,0:T(8,128)S(1)}, s32[1]{0:T(128)}) custom-call(f32[1]{0:T(128)S(6)} %copy.12.lr_hbm, f32[1]{0:T(128)S(6)} %copy.13.sr_hbm, s32[52,64,256]{2,1,0:T(8,128)} %ev_hbm.1, s32[64,256]{1,0:T(8,128)} %en_hbm.1, s32[64,256]{1,0:T(8,128)} %ex_hbm.1, f32[64,256]{1,0:T(8,128)} %lo_hbm.1, f32[64,256]{1,0:T(8,128)} %fr_hbm.1, ...), custom_call_target="tpu_custom_call" | custom-call | tf_op jit(solution)/shard_map/newton_fast/pallas_call | solution.py:702
  48.2 0.0 copy-done.5
  48.2 0.0 copy-done.4
  48.3 0.0 copy-done.3
  48.3 0.0 copy-done.2
  48.3 0.0 copy-done.1
  48.3 0.0 copy-done
  48.3 0.7 %slice_bitcast_fusion = (f32[64,256]{1,0:T(8,128)}, f32[64,256]{1,0:T(8,128)}) fusion(f32[2,64,256]{2,1,0:T(8,128)S(1)} %get-tuple-element.37), kind=kLoop, calls=%fused_computation | loop fusion | bytes 262144 | tf_op jit(solution)/shard_map/squeeze | solution.py:775
  (1 shorter events, 0.0 us)
Async XLA Ops:
  0.6 47.6 %copy-start.5 = (f32[64,256]{1,0:T(8,128)S(1)}, f32[64,256]{1,0:T(8,128)}, u32[]{:S(2)}) copy-start(f32[64,256]{1,0:T(8,128)} %ka_hbm.1) | copy-start | bytes 196612
  0.6 47.6 %copy-start.4 = (f32[64,256]{1,0:T(8,128)S(1)}, f32[64,256]{1,0:T(8,128)}, u32[]{:S(2)}) copy-start(f32[64,256]{1,0:T(8,128)} %fr_hbm.1) | copy-start | bytes 196612
  0.7 47.6 %copy-start.3 = (f32[64,256]{1,0:T(8,128)S(1)}, f32[64,256]{1,0:T(8,128)}, u32[]{:S(2)}) copy-start(f32[64,256]{1,0:T(8,128)} %lo_hbm.1) | copy-start | bytes 196612
  0.7 47.6 %copy-start.2 = (s32[64,256]{1,0:T(8,128)S(1)}, s32[64,256]{1,0:T(8,128)}, u32[]{:S(2)}) copy-start(s32[64,256]{1,0:T(8,128)} %ex_hbm.1) | copy-start | bytes 196612
  0.7 47.6 %copy-start.1 = (s32[64,256]{1,0:T(8,128)S(1)}, s32[64,256]{1,0:T(8,128)}, u32[]{:S(2)}) copy-start(s32[64,256]{1,0:T(8,128)} %en_hbm.1) | copy-start | bytes 196612
  0.7 47.6 %copy-start = (s32[52,64,256]{2,1,0:T(8,128)S(1)}, s32[52,64,256]{2,1,0:T(8,128)}, u32[]{:S(2)}) copy-start(s32[52,64,256]{2,1,0:T(8,128)} %ev_hbm.1) | copy-start | bytes 10223620
